TPU v7x, 32 devices: a whole 2x2x4 slice. The times are simulated.
32 devices in a mesh: emb: 16 (over z, y, x), dp: 2 (over core).
Axes of the slice: x: 2, y: 2, z: 4, core: 2. Of those that a mesh axis runs over, the one named last changes fastest.
Arguments:
- hashed_ids: int32 [256, 128], P(('emb', 'dp')), may hold values from 0 to 8191
- owners: int32 [256, 128, 1], P(('emb', 'dp')), may hold values from 0 to 15; in each aligned block of 1024 rows (0 to 1023, 1024 to 2047, ..., all dimensions but the last counted through in order) at most 128 rows name the same one
- domain_tags: int32 [256], P(('emb', 'dp')), may hold values from 0 to 2
- user_counts: int32 [3], replicated, may hold values from 512 to 8192
- lengths: int32 [32, 8], P(('emb', 'dp')), may hold values from 1 to 128, 640 in all within a row
- buckets: int32 [128, 128], replicated, may hold values from 0 to 31
- table: bfloat16 [524288, 128], P('emb'), may hold values from -6 to 6
- gain_one: float32 [128], replicated, may hold values from 0.5 to 1.5
- query_weight_matrix: bfloat16 [128, 384], replicated, may hold values from -0.5 to 0.5
- key_weight_matrix: bfloat16 [128, 384], replicated, may hold values from -0.5 to 0.5
- value_weight_matrix: bfloat16 [128, 384], replicated, may hold values from -0.5 to 0.5
- attention_output_weight: bfloat16 [384, 128], replicated, may hold values from -0.875 to 0.875
- bias_table: float32 [32, 6], replicated, may hold values from -4 to 4
- gain_two: float32 [128], replicated, may hold values from 0.5 to 1.5
- feedforward_input_weight: bfloat16 [128, 1024], replicated, may hold values from -0.5 to 0.5
- feedforward_output_weight: bfloat16 [1024, 128], replicated, may hold values from -0.1875 to 0.1875
- cotangent: bfloat16 [256, 128, 128], P(('emb', 'dp')), may hold values from -6 to 6
Outputs:
- output: bfloat16 [256, 128, 128], P(('emb', 'dp'))
- input_grad: float32 [256, 128, 128], P(('emb', 'dp'))
- table_grad: float32 [524288, 128], P('emb')
- gain_one_grad: float32 [128], replicated
- w_query_grad: float32 [128, 384], replicated
- w_key_grad: float32 [128, 384], replicated
- w_value_grad: float32 [128, 384], replicated
- w_output_grad: float32 [384, 128], replicated
- bias_grad: float32 [32, 6], replicated
- gain_two_grad: float32 [128], replicated
- w_in_grad: float32 [128, 1024], replicated
- w_out_grad: float32 [1024, 128], replicated
Inputs may be any that keep to these rules, and one draw needn't show every extreme that they name: `owners`: among the 1024 tokens of one device no shard is named more than 128 times, and in some device's tokens one shard is named exactly 128 times. The 8 lengths of each row sum to 640 and the largest of each row is 128.
All inputs are finite; a program needn't handle non-finite values.
Results may differ from a plain program's by a relative error of at most 0.012.
Values may be sent and summed in bfloat16 or wider, within the bound.
A program may use at most 128 MiB of HBM per device.

v0:
```python
import math

import jax
import jax.numpy as jnp
from jax import lax
from jax.sharding import PartitionSpec as P

DH = 64


epsilon = 1e-06
highest_precision = lax.Precision.HIGHEST


def norm_back(first_normalized, scale, grad_normed, gain):
    scaled = grad_normed * gain
    gain_grad = jnp.sum(grad_normed * first_normalized, axis=0)
    inner = jnp.mean(scaled * first_normalized, axis=-1, keepdims=True)
    return (scale * (scaled - first_normalized * inner), gain_grad)


def on_device(
    hashed_ids,
    owners,
    domain_tags,
    user_counts,
    lengths,
    buckets,
    table,
    gain_one,
    query_weight_matrix,
    key_weight_matrix,
    value_weight_matrix,
    attention_output_weight,
    bias_table,
    gain_two,
    feedforward_input_weight,
    feedforward_output_weight,
    cotangent,
):
    n_owner = lax.axis_size("emb")
    seq_count, length = hashed_ids.shape
    token_count = seq_count * length
    rows_dev, width = table.shape
    domain_rows = rows_dev // 4
    slot_cap = max(2, 2 * token_count // n_owner)
    heads = query_weight_matrix.shape[1] // DH
    bucket_count = bias_table.shape[0]
    root_scale = 1.0 / math.sqrt(DH)
    pick = (domain_tags[:, None] == jnp.arange(3, dtype=jnp.int32)[None, :]).astype(jnp.int32)
    counts = jnp.sum(pick * user_counts[None, :], axis=1)
    local = (domain_tags[:, None] * domain_rows + hashed_ids % counts[:, None]).reshape(token_count)
    owner_flat = owners.reshape(token_count)
    owner_hot = (owner_flat[:, None] == jnp.arange(n_owner, dtype=jnp.int32)[None, :]).astype(
        jnp.bfloat16
    )
    earlier = (jnp.arange(token_count)[:, None] > jnp.arange(token_count)[None, :]).astype(
        jnp.bfloat16
    )
    prefix = jnp.dot(earlier, owner_hot, preferred_element_type=jnp.float32)
    slot_index = jnp.sum(prefix * owner_hot.astype(jnp.float32), axis=1).astype(jnp.int32)
    position = owner_flat * slot_cap + slot_index
    requests = (
        jnp.full((n_owner * slot_cap,), rows_dev, jnp.int32)
        .at[position]
        .set(local)
        .reshape(n_owner, slot_cap)
    )
    asked = lax.all_to_all(requests, "emb", split_axis=0, concat_axis=0, tiled=True)
    safe_rows = jnp.minimum(asked, rows_dev - 1)
    found = jnp.where((asked < rows_dev)[..., None], table[safe_rows], jnp.zeros((), jnp.bfloat16))
    returned_rows = lax.all_to_all(found, "emb", split_axis=0, concat_axis=0, tiled=True)
    tokens_in = returned_rows.reshape(n_owner * slot_cap, width)[position]
    hidden_state_rows = tokens_in.astype(jnp.float32)
    bucket_hot = (
        buckets.reshape(length * length)[:, None]
        == jnp.arange(bucket_count, dtype=jnp.int32)[None, :]
    ).astype(jnp.float32)
    pair_bias = (
        jnp.dot(bucket_hot, bias_table, precision=highest_precision)
        .reshape(length, length, heads)
        .transpose(2, 0, 1)
    )
    visible = jnp.arange(length, dtype=jnp.int32)[None, :] < lengths[0][:, None]
    scale_one = lax.rsqrt(
        jnp.mean(hidden_state_rows * hidden_state_rows, axis=-1, keepdims=True) + epsilon
    )
    normed_one = hidden_state_rows * scale_one
    normed_in = (normed_one * gain_one).astype(jnp.bfloat16)
    query_rows = jnp.dot(normed_in, query_weight_matrix, preferred_element_type=jnp.float32).astype(
        jnp.bfloat16
    )
    key_matrix_full = jnp.dot(
        normed_in, key_weight_matrix, preferred_element_type=jnp.float32
    ).astype(jnp.bfloat16)
    value_matrix_full = jnp.dot(
        normed_in, value_weight_matrix, preferred_element_type=jnp.float32
    ).astype(jnp.bfloat16)
    head_q = query_rows.reshape(seq_count, length, heads, DH)
    head_k = key_matrix_full.reshape(seq_count, length, heads, DH)
    head_v = value_matrix_full.reshape(seq_count, length, heads, DH)

    def scores_of():
        raw = (
            jnp.einsum("sihd,sjhd->shij", head_q, head_k, preferred_element_type=jnp.float32)
            * root_scale
            + pair_bias[None]
        )
        return jnp.where(visible[:, None, None, :], raw, -1000000000.0)

    scores = scores_of()
    top_score = jnp.max(scores, axis=-1, keepdims=True)
    expo = jnp.exp(scores - top_score)
    total = jnp.sum(expo, axis=-1, keepdims=True)
    log_total = top_score + jnp.log(total)
    probs_low = (expo / total).astype(jnp.bfloat16)
    attention_mixture = jnp.einsum(
        "shij,sjhd->sihd", probs_low, head_v, preferred_element_type=jnp.float32
    )
    attention_mixture = attention_mixture.astype(jnp.bfloat16).reshape(token_count, heads * DH)
    residual_middle = hidden_state_rows + jnp.dot(
        attention_mixture, attention_output_weight, preferred_element_type=jnp.float32
    )
    scale_two = lax.rsqrt(
        jnp.mean(residual_middle * residual_middle, axis=-1, keepdims=True) + epsilon
    )
    second_normalized = residual_middle * scale_two
    normed_mid = (second_normalized * gain_two).astype(jnp.bfloat16)
    hidden_preactivation = jnp.dot(
        normed_mid, feedforward_input_weight, preferred_element_type=jnp.float32
    )
    activated_hidden = jax.nn.gelu(hidden_preactivation).astype(jnp.bfloat16)
    result = residual_middle + jnp.dot(
        activated_hidden, feedforward_output_weight, preferred_element_type=jnp.float32
    )
    output = result.astype(jnp.bfloat16).reshape(seq_count, length, width)
    live_rows = visible.reshape(token_count).astype(jnp.bfloat16)
    grad_y_low = cotangent.reshape(token_count, width) * live_rows[:, None]
    grad_y = grad_y_low.astype(jnp.float32)
    w_out_grad = jnp.einsum(
        "tf,td->fd", activated_hidden, grad_y_low, preferred_element_type=jnp.float32
    )
    grad_act = jnp.einsum(
        "td,fd->tf", grad_y_low, feedforward_output_weight, preferred_element_type=jnp.float32
    )
    _, gelu_back = jax.vjp(jax.nn.gelu, hidden_preactivation)
    grad_pre = gelu_back(grad_act)[0].astype(jnp.bfloat16)
    w_in_grad = jnp.einsum("td,tf->df", normed_mid, grad_pre, preferred_element_type=jnp.float32)
    grad_mid_norm = jnp.einsum(
        "tf,df->td", grad_pre, feedforward_input_weight, preferred_element_type=jnp.float32
    )
    grad_middle, gain_two_grad = norm_back(second_normalized, scale_two, grad_mid_norm, gain_two)
    grad_middle = grad_y + grad_middle
    grad_mid_low = grad_middle.astype(jnp.bfloat16)
    w_output_grad = jnp.einsum(
        "te,td->ed", attention_mixture, grad_mid_low, preferred_element_type=jnp.float32
    )
    grad_mixed = jnp.einsum(
        "td,ed->te", grad_mid_low, attention_output_weight, preferred_element_type=jnp.float32
    ).astype(jnp.bfloat16)
    head_grad = grad_mixed.reshape(seq_count, length, heads, DH)
    probs = jnp.exp(scores_of() - log_total)
    probs_again = probs.astype(jnp.bfloat16)
    grad_v = jnp.einsum(
        "shij,sihd->sjhd", probs_again, head_grad, preferred_element_type=jnp.float32
    ).astype(jnp.bfloat16)
    grad_probs = jnp.einsum(
        "sihd,sjhd->shij", head_grad, head_v, preferred_element_type=jnp.float32
    )
    grad_scores = (
        probs * (grad_probs - jnp.sum(grad_probs * probs, axis=-1, keepdims=True))
    ).astype(jnp.bfloat16)
    score_sum = (
        jnp.sum(grad_scores.astype(jnp.float32), axis=0)
        .transpose(1, 2, 0)
        .reshape(length * length, heads)
    )
    bias_grad = jnp.dot(bucket_hot.T, score_sum, precision=highest_precision)
    grad_q = (
        jnp.einsum("shij,sjhd->sihd", grad_scores, head_k, preferred_element_type=jnp.float32)
        * root_scale
    ).astype(jnp.bfloat16)
    grad_k = (
        jnp.einsum("shij,sihd->sjhd", grad_scores, head_q, preferred_element_type=jnp.float32)
        * root_scale
    ).astype(jnp.bfloat16)
    grad_q = grad_q.reshape(token_count, heads * DH)
    grad_k = grad_k.reshape(token_count, heads * DH)
    grad_v = grad_v.reshape(token_count, heads * DH)
    w_query_grad = jnp.einsum("td,te->de", normed_in, grad_q, preferred_element_type=jnp.float32)
    w_key_grad = jnp.einsum("td,te->de", normed_in, grad_k, preferred_element_type=jnp.float32)
    w_value_grad = jnp.einsum("td,te->de", normed_in, grad_v, preferred_element_type=jnp.float32)
    grad_normed = (
        jnp.einsum("te,de->td", grad_q, query_weight_matrix, preferred_element_type=jnp.float32)
        + jnp.einsum("te,de->td", grad_k, key_weight_matrix, preferred_element_type=jnp.float32)
        + jnp.einsum("te,de->td", grad_v, value_weight_matrix, preferred_element_type=jnp.float32)
    )
    grad_states, gain_one_grad = norm_back(normed_one, scale_one, grad_normed, gain_one)
    grad_states = grad_middle + grad_states
    input_grad = grad_states.reshape(seq_count, length, width)
    outgoing = jnp.zeros((n_owner * slot_cap, width), jnp.float32).at[position].set(grad_states)
    incoming = lax.all_to_all(
        outgoing.reshape(n_owner, slot_cap, width).astype(jnp.bfloat16),
        "emb",
        split_axis=0,
        concat_axis=0,
        tiled=True,
    ).astype(jnp.float32)
    empty_grad = jnp.zeros((rows_dev, width), jnp.float32)
    partial_grad = empty_grad.at[asked.reshape(-1)].add(incoming.reshape(-1, width), mode="drop")
    table_grad = lax.psum(partial_grad.astype(jnp.bfloat16), "dp").astype(jnp.float32)
    summed = lax.psum(
        (
            gain_one_grad,
            w_query_grad,
            w_key_grad,
            w_value_grad,
            w_output_grad,
            bias_grad,
            gain_two_grad,
            w_in_grad,
            w_out_grad,
        ),
        ("emb", "dp"),
    )
    return (
        output,
        input_grad,
        table_grad,
        summed[0],
        summed[1],
        summed[2],
        summed[3],
        summed[4],
        summed[5],
        summed[6],
        summed[7],
        summed[8],
    )


def solution(mesh):
    return jax.shard_map(
        on_device,
        mesh=mesh,
        in_specs=(
            P(("emb", "dp"), None),
            P(("emb", "dp"), None, None),
            P(("emb", "dp")),
            P(),
            P(("emb", "dp"), None),
            P(),
            P("emb", None),
            P(),
            P(),
            P(),
            P(),
            P(),
            P(),
            P(),
            P(),
            P(),
            P(("emb", "dp"), None, None),
        ),
        out_specs=(
            P(("emb", "dp"), None, None),
            P(("emb", "dp"), None, None),
            P("emb", None),
            P(),
            P(),
            P(),
            P(),
            P(),
            P(),
            P(),
            P(),
            P(),
        ),
        check_vma=False,
    )
```

profile of v0, /device:TPU:27, one launch (start us, length us, event | category | flops | bytes accessed | tf_op | source)
XLA Modules:
  0.0 341.5 jit_solution(4820154699032195319)
XLA Ops:
  8.7 1.3 fusion.31
  10.7 0.9 fusion.87
  11.5 4.3 %scatter_custom_fusion = s32[2048]{0:T(1024)S(1)} fusion(s32[1024]{0:T(1024)S(1)} %bitcast.176, s32[1024]{0:T(1024)S(1)} %fusion.87, s32[]{:T(128)} %constant.20.clone.1), kind=kCustom, calls=%fused_computation.132 | custom fusion | bytes 8196 | tf_op jit(solution)/shard_map/scatter | solution.py:66
  15.9 8.6 %all_to_all.19 = s32[16,1,128]{2,1,0:T(1,128)S(1)} all-to-all(s32[16,1,128]{2,1,0:T(1,128)S(1)} %bitcast.174), channel_id=1, replica_groups=mesh['emb'=16,'dp'=2] {'emb'}, dimensions={0} | all-to-all | bytes 16384 | tf_op jit(solution)/shard_map/all_to_all | solution.py:69
  24.5 10.1 %gather_fusion = bf16[2048,128]{1,0:T(8,128)(2,1)S(1)} fusion(bf16[32768,128]{1,0:T(8,128)(2,1)} %param.23, s32[2048]{0:T(1024)S(1)} %fusion.85), kind=kCustom, calls=%fused_computation | custom fusion | bytes 1056768 | tf_op jit(solution)/shard_map/gather | solution.py:71
  34.6 1.1 broadcast_select_fusion
  35.8 7.4 %all-to-all-start.1 = ((bf16[16,128,128]{2,1,0:T(8,128)(2,1)}), bf16[16,128,128]{2,1,0:T(8,128)(2,1)S(1)}, u32[]{:S(2)}, u32[]{:S(2)}) async-start(bf16[16,128,128]{2,1,0:T(8,128)(2,1)} %broadcast_select_fusion), calls=%async_computation.1 | async-start | bytes 1048576 | tf_op jit(solution)/shard_map/all_to_all | solution.py:72
  44.0 0.9 copy.113
  45.0 0.9 bitcast_multiply_fusion
  45.9 8.2 %all-to-all-done.1 = bf16[16,128,128]{2,1,0:T(8,128)(2,1)S(1)} async-done(((bf16[16,128,128]{2,1,0:T(8,128)(2,1)}), bf16[16,128,128]{2,1,0:T(8,128)(2,1)S(1)}, u32[]{:S(2)}, u32[]{:S(2)}) %all-to-all-start.1) | async-done | bytes 524320 | tf_op jit(solution)/shard_map/all_to_all | solution.py:72
  54.2 3.2 gather_fusion.1
  58.4 1.1 copy.136
  60.2 1.1 copy.135
  62.2 2.8 fusion.98
  67.6 2.9 multiply_convert_fusion
  70.5 3.4 fusion.8
  73.9 1.3 copy-done.6
  75.2 1.2 multiply_reduce_fusion.1
  77.8 1.3 convolution_convert_fusion
  79.0 2.3 copy.117
  81.3 1.4 copy.139
  82.7 1.2 fusion.23
  83.9 1.0 multiply_reduce_fusion
  84.9 1.8 convert_reduce_fusion
  86.7 1.2 fusion.27
  92.1 3.5 %scatter_custom_fusion.1 = f32[2048,128]{1,0:T(8,128)S(1)} fusion(s32[1024]{0:T(1024)} %bitcast.178, f32[1024,128]{1,0:T(8,128)S(1)} %fusion.73, f32[]{:T(128)} %constant.22.clone.1), kind=kCustom, calls=%fused_computation.103 | custom fusion | bytes 1049088 | tf_op jit(solution)/shard_map/scatter | solution.py:201
  96.4 6.7 %all-to-all-start.2 = ((bf16[16,128,128]{2,1,0:T(8,128)(2,1)}), bf16[16,128,128]{2,1,0:T(8,128)(2,1)S(1)}, u32[]{:S(2)}, u32[]{:S(2)}) async-start(bf16[16,128,128]{2,1,0:T(8,128)(2,1)} %bitcast.25), calls=%async_computation.2 | async-start | bytes 1048576 | tf_op jit(solution)/shard_map/all_to_all | solution.py:202
  103.5 10.7 %all-to-all-done.2 = bf16[16,128,128]{2,1,0:T(8,128)(2,1)S(1)} async-done(((bf16[16,128,128]{2,1,0:T(8,128)(2,1)}), bf16[16,128,128]{2,1,0:T(8,128)(2,1)S(1)}, u32[]{:S(2)}, u32[]{:S(2)}) %all-to-all-start.2) | async-done | bytes 524320 | tf_op jit(solution)/shard_map/all_to_all | solution.py:202
  114.1 18.7 %scatter_custom_fusion.2 = f32[32768,128]{1,0:T(8,128)} fusion(s32[2048]{0:T(1024)S(1)} %bitcast.180, f32[]{:T(128)} %constant.22.clone.1, bf16[2048,128]{1,0:T(8,128)(2,1)S(1)} %bitcast.161), kind=kCustom, calls=%fused_computation.5 | custom fusion | flops 524288 | bytes 17301508 | tf_op jit(solution)/shard_map/scatter-add | solution.py:210
  132.8 8.9 %convert_element_type.148 = bf16[32768,128]{1,0:T(8,128)(2,1)} convert(f32[32768,128]{1,0:T(8,128)} %scatter_custom_fusion.2) | non-fusion elementwise | flops 4194304 | bytes 25165824 | tf_op jit(solution)/shard_map/convert_element_type | solution.py:211
  141.8 2.6 fusion.35
  144.3 2.4 fusion.38
  146.7 2.4 fusion.41
  149.2 1.0 fusion.45
  150.2 1.5 fusion.99
  151.8 1.5 fusion.90
  153.4 0.9 copy.129
  154.3 2.2 fusion.12
  156.5 41.6 %all-reduce = (f32[128]{0:T(128)}, f32[32,6]{0,1:T(8,128)}, f32[128]{0:T(128)}) all-reduce(f32[128]{0:T(128)S(1)} %get-tuple-element.14, f32[32,6]{0,1:T(8,128)S(1)} %fusion.12, f32[128]{0:T(128)S(1)} %copy-done.45), channel_id=1, replica_groups=mesh['emb'=16,'dp'=2] {'emb','dp'}, use_global_device_ids=true, to_apply=%region_14.15 | all-reduce | flops 448 | bytes 3584 | tf_op jit(solution)/shard_map/psum | solution.py:212
  198.1 1.4 fusion.29
  199.5 9.6 %convert_element_type.149 = f32[32768,128]{1,0:T(8,128)} convert(bf16[32768,128]{1,0:T(8,128)(2,1)} %all-reduce.5.cloned.1.call-done) | non-fusion elementwise | flops 4194304 | bytes 25165824 | tf_op jit(solution)/shard_map/convert_element_type | solution.py:211
  209.1 115.3 %all-reduce.7.cloned.1.call-done = (f32[128,384]{1,0:T(8,128)}, f32[128,384]{1,0:T(8,128)}, f32[128,384]{1,0:T(8,128)}, f32[384,128]{1,0:T(8,128)}, f32[128,1024]{1,0:T(8,128)}, /*index=5*/f32[1024,128]{1,0:T(8,128)}) async-done(((f32[128,384]{1,0:T(8,128)}, f32[128,384]{1,0:T(8,128)}, f32[128,384]{1,0:T(8,128)}, f32[384,128]{1,0:T(8,128)}, f32[128,1024]{1,0:T(8,128)}, /*index=5*/f32[1024,128]{1,0:T(8,128)}), ...) | async-done | bytes 1835024 | tf_op jit(solution)/shard_map/psum | solution.py:212
  324.4 1.6 copy.217
  326.1 1.6 copy.218
  327.7 1.6 copy.219
  329.3 1.6 copy.220
  330.9 1.9 copy.221
  332.8 1.9 copy.222
  (138 shorter events, 14.7 us)
Async XLA Ops:
  7.2 60.4 %copy-start = (bf16[128,1024]{1,0:T(8,128)(2,1)S(1)}, bf16[128,1024]{1,0:T(8,128)(2,1)}, u32[]{:S(2)}) copy-start(bf16[128,1024]{1,0:T(8,128)(2,1)} %param.31) | copy-start | bytes 786436
  10.6 34.4 %copy-start.39 = (s32[1024,1]{0,1:T(1,128)}, s32[1024,1]{0,1:T(1,128)S(1)}, u32[]{:S(2)}) copy-start(s32[1024,1]{0,1:T(1,128)S(1)} %compare_select_fusion.1) | copy-start | bytes 12292
  24.5 18.7 %copy-start.35 = (s32[128,128]{1,0:T(8,128)S(1)}, s32[128,128]{1,0:T(8,128)}, u32[]{:S(2)}) copy-start(s32[128,128]{1,0:T(8,128)} %param.22) | copy-start | bytes 196612
  24.5 18.7 %copy-start.44 = (f32[32,6]{0,1:T(8,128)S(1)}, f32[32,6]{0,1:T(8,128)}, u32[]{:S(2)}) copy-start(f32[32,6]{0,1:T(8,128)} %param.29) | copy-start | bytes 2308
  34.6 10.3 %copy-start.46 = (s32[1,8]{1,0:T(1,128)S(1)}, s32[1,8]{1,0:T(1,128)}, u32[]{:S(2)}) copy-start(s32[1,8]{1,0:T(1,128)} %param.21) | copy-start | bytes 100
  34.6 10.4 %copy-start.21 = (bf16[8,128,128]{2,1,0:T(8,128)(2,1)S(1)}, bf16[8,128,128]{2,1,0:T(8,128)(2,1)}, u32[]{:S(2)}) copy-start(bf16[8,128,128]{2,1,0:T(8,128)(2,1)} %param.33) | copy-start | bytes 786436
  35.8 21.9 %copy-start.28 = (bf16[128,384]{1,0:T(8,128)(2,1)S(1)}, bf16[128,384]{1,0:T(8,128)(2,1)}, u32[]{:S(2)}) copy-start(bf16[128,384]{1,0:T(8,128)(2,1)} %param.26) | copy-start | bytes 294916
  35.8 21.9 %copy-start.40 = (f32[128]{0:T(128)S(1)}, f32[128]{0:T(128)}, u32[]{:S(2)}) copy-start(f32[128]{0:T(128)} %param.24) | copy-start | bytes 1540
  35.8 18.4 %all-to-all-start.1 = ((bf16[16,128,128]{2,1,0:T(8,128)(2,1)}), bf16[16,128,128]{2,1,0:T(8,128)(2,1)S(1)}, u32[]{:S(2)}, u32[]{:S(2)}) async-start(bf16[16,128,128]{2,1,0:T(8,128)(2,1)} %broadcast_select_fusion), calls=%async_computation.1 | async-start | bytes 1048576 | tf_op jit(solution)/shard_map/all_to_all | solution.py:72
  45.0 9.2 %copy-start.37 = (bf16[1024]{0:T(1024)(128)(2,1)}, bf16[1024]{0:T(1024)(128)(2,1)S(1)}, u32[]{:S(2)}) copy-start(bf16[1024]{0:T(1024)(128)(2,1)S(1)} %get-tuple-element.27) | copy-start | bytes 6148
  54.2 5.3 %copy-start.27 = (bf16[128,384]{1,0:T(8,128)(2,1)S(1)}, bf16[128,384]{1,0:T(8,128)(2,1)}, u32[]{:S(2)}) copy-start(bf16[128,384]{1,0:T(8,128)(2,1)} %param.25) | copy-start | bytes 294916
  57.4 3.9 %copy-start.3 = (bf16[1024,128]{1,0:T(8,128)(2,1)}, bf16[1024,128]{1,0:T(8,128)(2,1)S(1)}, u32[]{:S(2)}) copy-start(bf16[1024,128]{1,0:T(8,128)(2,1)S(1)} %gather_fusion.1) | copy-start | bytes 786436
  58.4 2.9 copy-start.32
  62.2 3.6 %copy-start.18 = (bf16[48,8,8,128]{3,2,1,0:T(8,128)(2,1)}, bf16[48,8,8,128]{3,2,1,0:T(8,128)(2,1)S(1)}, u32[]{:S(2)}) copy-start(bf16[48,8,8,128]{3,2,1,0:T(8,128)(2,1)S(1)} %copy.134) | copy-start | bytes 2359300
  65.8 1.3 copy-start.4
  65.8 1.3 copy-start.34
  67.0 3.5 %copy-start.12 = (bf16[8,128,6,64]{1,0,3,2:T(8,128)(2,1)}, bf16[8,128,6,64]{1,0,3,2:T(8,128)(2,1)S(1)}, u32[]{:S(2)}) copy-start(bf16[8,128,6,64]{1,0,3,2:T(8,128)(2,1)S(1)} %copy.116) | copy-start | bytes 2359300
  67.6 8.9 %copy-start.8 = (f32[1024,128]{1,0:T(8,128)}, f32[1024,128]{1,0:T(8,128)S(1)}, u32[]{:S(2)}) copy-start(f32[1024,128]{1,0:T(8,128)S(1)} %get-tuple-element.32) | copy-start | bytes 1572868
  67.6 2.9 copy-start.23
  67.6 2.9 copy-start.30
  73.9 1.3 copy-start.6
  75.2 1.2 copy-start.22
  75.2 1.2 copy-start.38
  81.3 2.6 copy-start.19
  84.9 1.8 copy-start.15
  88.5 2.1 copy-start.29
  89.0 2.0 copy-start.25
  89.0 2.0 copy-start.5
  89.0 2.0 copy-start.33
  89.0 2.0 copy-start.41
  89.6 2.1 copy-start.16
  90.1 1.6 copy-start.17
  90.1 1.6 copy-start.11
  92.0 40.8 %copy-start.26 = (f32[1024,128]{1,0:T(8,128)}, f32[1024,128]{1,0:T(8,128)S(1)}, u32[]{:S(2)}) copy-start(f32[1024,128]{1,0:T(8,128)S(1)} %fusion.73) | copy-start | bytes 1572868
  96.4 17.7 %all-to-all-start.2 = ((bf16[16,128,128]{2,1,0:T(8,128)(2,1)}), bf16[16,128,128]{2,1,0:T(8,128)(2,1)S(1)}, u32[]{:S(2)}, u32[]{:S(2)}) async-start(bf16[16,128,128]{2,1,0:T(8,128)(2,1)} %bitcast.25), calls=%async_computation.2 | async-start | bytes 1048576 | tf_op jit(solution)/shard_map/all_to_all | solution.py:202
  103.1 96.4 %all-reduce.5.cloned.1.call-start = ((), (), s32[]{:S(2)}) async-start(), calls=%async_computation.3 | async-start | bytes 16777216 | tf_op jit(solution)/shard_map/psum | solution.py:211
  141.7 8.5 %copy-start.2 = (bf16[1024,1024]{1,0:T(8,128)(2,1)S(1)}, bf16[1024,1024]{1,0:T(8,128)(2,1)}, u32[]{:S(2)}) copy-start(bf16[1024,1024]{1,0:T(8,128)(2,1)} %get-tuple-element.33) | copy-start | bytes 6291460
  141.7 182.7 %all-reduce.7.cloned.1.call-start = ((), (), s32[]{:S(2)}) async-start(), calls=%async_computation.4 | async-start | bytes 3670016 | tf_op jit(solution)/shard_map/psum | solution.py:212
  141.8 7.4 %copy-start.13 = (bf16[8,128,6,64]{1,0,3,2:T(8,128)(2,1)S(1)}, bf16[8,128,6,64]{1,0,3,2:T(8,128)(2,1)}, u32[]{:S(2)}) copy-start(bf16[8,128,6,64]{1,0,3,2:T(8,128)(2,1)} %copy-done.12) | copy-start | bytes 2359300
  141.8 8.4 %copy-start.24 = (bf16[1024,128]{1,0:T(8,128)(2,1)S(1)}, bf16[1024,128]{1,0:T(8,128)(2,1)}, u32[]{:S(2)}) copy-start(bf16[1024,128]{1,0:T(8,128)(2,1)} %bitcast_multiply_fusion) | copy-start | bytes 786436
  149.1 2.6 copy-start.7
  149.1 2.6 copy-start.9
  149.2 2.6 copy-start.43
  151.8 1.6 copy-start.20
  151.8 2.5 copy-start.36
  151.8 4.7 %copy-start.45 = (f32[128]{0:T(128)S(1)}, f32[128]{0:T(128)}, u32[]{:S(2)}) copy-start(f32[128]{0:T(128)} %get-tuple-element.12) | copy-start | bytes 1540
  151.8 46.3 %copy-start.31 = (bf16[1024,128]{1,0:T(8,128)(2,1)S(1)}, bf16[1024,128]{1,0:T(8,128)(2,1)}, u32[]{:S(2)}) copy-start(bf16[1024,128]{1,0:T(8,128)(2,1)} %param.32) | copy-start | bytes 786436
  199.5 135.1 %copy-start.1 = (bf16[128,1024]{1,0:T(8,128)(2,1)S(1)}, bf16[128,1024]{1,0:T(8,128)(2,1)}, u32[]{:S(2)}) copy-start(bf16[128,1024]{1,0:T(8,128)(2,1)} %param.31) | copy-start | bytes 786436
  (3 other events, 3.1 us)
Sparse Core Ops, SparseCore 0:
  141.8 42.2 all-reduce.4
  191.6 132.7 all-reduce.6
where the time goes:
time: 348 us; the launch traced here: 342 us
  waiting for transfers between devices  134 us (39%)
  blocking collectives  50.2 us (14%)
  other arithmetic  46.8 us (13%)
  local copies, waits for them, and re-layouts  44.5 us (13%)
  matrix products  36.5 us (10%)
  between operations  14.8 us (4%)
  starting transfers between devices  14.5 us (4%)
    psum x1, waiting for transfers between devices, on_device(): lax.psum((gain_one_grad, w_query_grad, w_key_grad, w_value_grad, w_output...  115 us
    psum x1, blocking collectives, on_device(): lax.psum((gain_one_grad, w_query_grad, w_key_grad, w_value_grad, w_output...  41.6 us
    scatter-add x1, other arithmetic, on_device(): empty_grad.at[asked.reshape(-1)]  18.7 us
    unnamed x105, local copies, waits for them, and re-layouts  16.4 us
    all_to_all x1, waiting for transfers between devices, on_device(): lax.all_to_all(outgoing.reshape(n_owner, slot_cap, width).astype(jnp.bflo...  10.7 us
    gather x1, local copies, waits for them, and re-layouts, on_device(): table[safe_rows]  10.1 us
    convert_element_type x1, other arithmetic, on_device(): lax.psum(partial_grad.astype(jnp.bfloat16), 'dp').astype(jnp.float32)  9.6 us
    convert_element_type x1, other arithmetic, on_device(): partial_grad.astype(jnp.bfloat16)  8.86 us
  transfers between devices with their start and end apart: 4, of which 3 were waited for; matrix products, arithmetic and copies ran while one was open for 8% of the time, Pallas kernels for 0%

commit v1 on v0

v1 whole, which is shorter than its diff:
```python
import functools
import math

import jax
import jax.numpy as jnp
from jax import lax
from jax.experimental import pallas as pl
from jax.experimental.pallas import tpu as pltpu
from jax.sharding import PartitionSpec as P

DH = 64
LANES = 128
EPSILON = 1e-06
LIVE = 32768
MESH = pl.DeviceIdType.MESH
F32 = jnp.float32
BF16 = jnp.bfloat16
VMEM_LIMIT = 56 * 1024 * 1024


def dot_nn(a, b):
    return lax.dot_general(a, b, (((1,), (0,)), ((), ())), preferred_element_type=F32)


def dot_nt(a, b):
    return lax.dot_general(a, b, (((1,), (1,)), ((), ())), preferred_element_type=F32)


def dot_tn(a, b):
    return lax.dot_general(a, b, (((0,), (0,)), ((), ())), preferred_element_type=F32)


def hot_slots(pos, first, count):
    rows = lax.broadcasted_iota(jnp.int32, (count, LANES), 0) + first
    parts = [
        jnp.where(rows == pos[s : s + 1, :], 1.0, 0.0).astype(BF16) for s in range(pos.shape[0])
    ]
    return jnp.concatenate(parts, axis=1)


def lookup_body(
    n, cap, used, ids, own, tags, counts, lens, table,
    x_t, pos_out, asked_out,
    req, asked_v, asked_s, tab_low, tab, gbuf, send, recv, x_acc,
    req_send, req_recv, row_send, row_recv, pair_send, pair_recv, tab_sem, smem_sem,
):
    me = lax.axis_index("emb")
    core = lax.axis_index("dp")
    seqs, length = ids.shape
    domain_rows = used // 3
    pieces = tab_sem.shape[0]
    piece = used // pieces

    barrier = pltpu.get_barrier_semaphore()

    def greet(k, carry):
        pl.semaphore_signal(
            barrier, inc=1, device_id={"emb": lax.rem(me + k, n)}, device_id_type=MESH
        )
        return carry

    lax.fori_loop(1, n, greet, 0)
    pl.semaphore_signal(barrier, inc=1, device_id={"dp": 1 - core}, device_id_type=MESH)

    def table_copy(c):
        part = pl.ds(c * piece, piece)
        return pltpu.make_async_copy(table.at[part], tab_low.at[part], tab_sem.at[c])

    for c in range(pieces):
        table_copy(c).start()

    row_id = lax.broadcasted_iota(jnp.int32, (seqs, length), 0)
    lane_id = lax.broadcasted_iota(jnp.int32, (seqs, length), 1)
    count_of = jnp.zeros((seqs, length), F32)
    tag_of = jnp.zeros((seqs, length), jnp.int32)
    len_of = jnp.zeros((seqs, length), jnp.int32)
    for s in range(seqs):
        tag = tags[s]
        count_of = jnp.where(row_id == s, counts[tag].astype(F32), count_of)
        tag_of = jnp.where(row_id == s, tag, tag_of)
        len_of = jnp.where(row_id == s, lens[0, s], len_of)
    code = ids[...].astype(F32)
    turns = jnp.floor((code + 0.5) / jnp.maximum(count_of, 1.0))
    local = tag_of * domain_rows + (code - turns * count_of).astype(jnp.int32)
    live = lane_id < len_of
    rel = own[...] - me
    rel = jnp.where(rel < 0, rel + n, rel)

    owner_id = lax.broadcasted_iota(jnp.int32, (n, length), 0)
    hot_live, hot_dead = [], []
    for s in range(seqs):
        hot = owner_id == rel[s : s + 1, :]
        alive = jnp.broadcast_to(live[s : s + 1, :].astype(F32), (n, length))
        hot_live.append(jnp.where(hot, alive, 0.0))
        hot_dead.append(jnp.where(hot, 1.0 - alive, 0.0))
    both = jnp.concatenate(hot_live + hot_dead, axis=0).astype(BF16)
    before = (
        lax.broadcasted_iota(jnp.int32, (length, length), 0)
        < lax.broadcasted_iota(jnp.int32, (length, length), 1)
    )
    prefix = dot_nn(both, jnp.where(before, 1.0, 0.0).astype(BF16))
    running = jnp.zeros((n, 1), F32)
    ranks = []
    for part, hots in enumerate((hot_live, hot_dead)):
        for s in range(seqs):
            at = (part * seqs + s) * n
            ranks.append(
                jnp.sum(hots[s] * (prefix[at : at + n] + running), axis=0, keepdims=True)
            )
            running = running + jnp.sum(hots[s], axis=1, keepdims=True)
    rank = jnp.concatenate([ranks[s] + ranks[seqs + s] for s in range(seqs)], axis=0)
    rank = rank.astype(jnp.int32)
    pos = rel * cap + rank
    pos_out[...] = pos

    low = (local & 255).astype(F32)
    high = (lax.shift_right_logical(local, 8) + jnp.where(live, LIVE // 256, 0)).astype(F32)
    slot_id = lax.broadcasted_iota(jnp.int32, (LANES, length), 0)
    asking = jnp.zeros((2 * n, LANES), F32)
    for s in range(seqs):
        hot = hot_live[s] + hot_dead[s]
        values = jnp.concatenate([hot * high[s : s + 1, :], hot * low[s : s + 1, :]], axis=0)
        slot_hot = jnp.where(slot_id == rank[s : s + 1, :], 1.0, 0.0).astype(BF16)
        asking = asking + dot_nt(values.astype(BF16), slot_hot)
    wanted = (asking[:n] * 256.0 + asking[n:]).astype(jnp.int32)
    for j in range(n):
        req[j] = wanted[j : j + 1, :]

    pl.semaphore_wait(barrier, n)

    def request(j):
        back = lax.rem(n - j, n)
        return pltpu.make_async_remote_copy(
            src_ref=req.at[j],
            dst_ref=asked_v.at[back],
            send_sem=req_send.at[j],
            recv_sem=req_recv.at[back],
            device_id={"emb": lax.rem(me + j, n)},
            device_id_type=MESH,
        )

    def arrived(j):
        return pltpu.make_async_remote_copy(
            src_ref=req.at[j],
            dst_ref=asked_v.at[j],
            send_sem=req_send.at[j],
            recv_sem=req_recv.at[j],
            device_id={"emb": lax.rem(me + j, n)},
            device_id_type=MESH,
        )

    def ask(j, carry):
        request(j).start()
        return carry

    lax.fori_loop(1, n, ask, 0)
    asked_v[0] = req[0]

    for c in range(pieces):
        table_copy(c).wait()

        def widen(r, carry):
            part = pl.ds(pl.multiple_of(c * piece + r * 256, 256), 256)
            tab[part, :] = tab_low[part, :].astype(F32)
            return carry

        lax.fori_loop(0, piece // 256, widen, 0)

    def all_asked(j, carry):
        arrived(j).wait_recv()
        return carry

    lax.fori_loop(1, n, all_asked, 0)
    to_scalar = pltpu.make_async_copy(asked_v, asked_s, smem_sem)
    to_scalar.start()

    def tally(j, carry):
        values = asked_v[j]
        asked_out[core, j, 0:1] = values
        number = jnp.sum(jnp.where(values >= LIVE, 1.0, 0.0), axis=1, keepdims=True)
        asked_out[core, j, 1:2] = jnp.broadcast_to(number.astype(jnp.int32), (1, LANES))
        return carry

    lax.fori_loop(0, n, tally, 0)
    share = pltpu.make_async_remote_copy(
        src_ref=asked_out.at[core],
        dst_ref=asked_out.at[core],
        send_sem=pair_send,
        recv_sem=pair_recv,
        device_id={"dp": 1 - core},
        device_id_type=MESH,
    )
    share.start()
    to_scalar.wait()

    def row_copy(j):
        back = lax.rem(n - j, n)
        return pltpu.make_async_remote_copy(
            src_ref=send.at[pl.ds(pl.multiple_of(j * cap, cap), cap)],
            dst_ref=recv.at[pl.ds(pl.multiple_of(back * cap, cap), cap)],
            send_sem=row_send.at[j],
            recv_sem=row_recv.at[back],
            device_id={"emb": lax.rem(me + j, n)},
            device_id_type=MESH,
        )

    def row_arrival(j):
        part = pl.ds(pl.multiple_of(j * cap, cap), cap)
        return pltpu.make_async_remote_copy(
            src_ref=send.at[part],
            dst_ref=recv.at[part],
            send_sem=row_send.at[j],
            recv_sem=row_recv.at[j],
            device_id={"emb": lax.rem(me + j, n)},
            device_id_type=MESH,
        )

    def gather(j):
        def eight(c, carry):
            for r in range(8):
                at = jnp.minimum(asked_s[j, 0, c * 8 + r] & (LIVE - 1), used - 1)
                gbuf[pl.ds(c * 8 + r, 1), :] = tab[pl.ds(at, 1), :]
            return carry

        lax.fori_loop(0, cap // 8, eight, 0)
        return gbuf[...].astype(BF16)

    def serve(j, carry):
        send[pl.ds(pl.multiple_of(j * cap, cap), cap), :] = gather(j)
        row_copy(j).start()
        return carry

    lax.fori_loop(1, n, serve, 0)
    recv[0:cap, :] = gather(0)

    def place(pair, carry):
        def ready(j, inner):
            row_arrival(j).wait_recv()
            return inner

        lax.fori_loop(jnp.maximum(2 * pair, 1), 2 * pair + 2, ready, 0)
        first = pl.multiple_of(pair * 2 * cap, 2 * cap)
        hot = hot_slots(pos_out[...], first, 2 * cap)
        got = dot_tn(recv[pl.ds(first, 2 * cap), :], hot)

        @pl.when(pair == 0)
        def _():
            x_acc[...] = got

        @pl.when(pair > 0)
        def _():
            x_acc[...] += got

        return carry

    lax.fori_loop(0, n // 2, place, 0)
    x_t[...] = x_acc[...].astype(BF16)

    def sent(j, carry):
        request(j).wait_send()
        row_copy(j).wait_send()
        return carry

    lax.fori_loop(1, n, sent, 0)
    share.wait()


def gelu_parts(u):
    k0 = math.sqrt(2.0 / math.pi)
    k1 = k0 * 0.044715
    square = u * u
    half = 0.5 * jnp.tanh(u * (k1 * square + k0)) + 0.5
    value = u * half
    slope = half + (2.0 * value) * (1.0 - half) * (3.0 * k1 * square + k0)
    return value, slope


def split_pair(both):
    zero = jnp.zeros((DH, LANES), both.dtype)
    left = jnp.concatenate([both[:DH], zero], axis=0)
    right = jnp.concatenate([zero, both[DH:]], axis=0)
    return jnp.concatenate([left, right], axis=1)


def block_body(
    cap2, lens, btab, buckets, x_t, cot, g1, wq, wk, wv, wo, g2, win, wout, pos,
    y_out, ig_out, slots_out, w_out, small_out,
    wqkv_t, wqkv, wo_t, win_t, wout_t, buck_t, bias, a_t, qkv_t, kv, p_s, o_t, c_t, act_t, du_t,
    dy_t, dm_t, dmb_t, do_t, dqkv_t, dsum, igb_t, g1_acc, g2_acc, b_acc,
):
    seqs, length, width = cot.shape
    tokens = seqs * length
    hd = wq.shape[1]
    ff = win.shape[1]
    heads = hd // DH
    pairs = heads // 2
    chunk = 256
    chunks = tokens // chunk
    bucket_count = btab.shape[1]

    for part, w in enumerate((wq, wk, wv)):
        wqkv[:, part * hd : (part + 1) * hd] = w[...]
        wqkv_t[part * hd : (part + 1) * hd, :] = w[...].T
    wo_t[...] = wo[...].T
    win_t[...] = win[...].T
    wout_t[...] = wout[...].T
    buck_t[...] = buckets[...].astype(F32).T
    g1_col = jnp.broadcast_to(g1[...], (8, width)).T[:, 0:1]
    g2_col = jnp.broadcast_to(g2[...], (8, width)).T[:, 0:1]
    g1_acc[...] = jnp.zeros_like(g1_acc)
    g2_acc[...] = jnp.zeros_like(g2_acc)
    dsum[...] = jnp.zeros_like(dsum)
    b_acc[...] = jnp.zeros_like(b_acc)

    def bias_rows(r, carry):
        part = pl.ds(pl.multiple_of(r * 8, 8), 8)
        bt = buck_t[part, :]
        rows = [jnp.zeros((8, length), F32) for _ in range(heads)]
        for b in range(bucket_count):
            here = bt == float(b)
            rows = [jnp.where(here, btab[h, b], rows[h]) for h in range(heads)]
        for p in range(pairs):
            bias[p, part, :] = jnp.concatenate(rows[2 * p : 2 * p + 2], axis=1)
        return carry

    lax.fori_loop(0, length // 8, bias_rows, 0)

    def norm_one(c):
        xf = x_t[:, pl.ds(pl.multiple_of(c * chunk, chunk), chunk)].astype(F32)
        scale = lax.rsqrt(jnp.mean(xf * xf, axis=0, keepdims=True) + EPSILON)
        return xf, scale

    def project(c, carry):
        part = pl.ds(pl.multiple_of(c * chunk, chunk), chunk)
        xf, scale = norm_one(c)
        a = (xf * scale * g1_col).astype(BF16)
        a_t[:, part] = a
        out = dot_nn(wqkv_t[...], a)
        qkv_t[0:hd, part] = out[:hd].astype(BF16) * jnp.array(1.0 / math.sqrt(DH), BF16)
        qkv_t[hd:, part] = out[hd:].astype(BF16)
        kv[part, :] = dot_nn(a.T, wqkv[:, hd:]).astype(BF16)
        return carry

    lax.fori_loop(0, chunks, project, 0)

    def attend(s, carry):
        part = pl.ds(pl.multiple_of(s * length, length), length)
        visible = lax.broadcasted_iota(jnp.int32, (length, 2 * length), 0) < lens[0, s]
        alive = lax.broadcasted_iota(jnp.int32, (width, length), 1) < lens[0, s]
        dy_t[:, part] = jnp.where(alive, cot[s].astype(F32).T, 0.0).astype(BF16)
        for p in range(pairs):
            rows = slice(p * 2 * DH, (p + 1) * 2 * DH)
            scores = dot_nn(kv[part, rows], split_pair(qkv_t[rows, part])) + bias[p]
            scores = jnp.where(visible, scores, -1000000000.0)
            expo = jnp.exp(scores - jnp.max(scores, axis=0, keepdims=True))
            prob = expo * (1.0 / jnp.sum(expo, axis=0, keepdims=True))
            p_s[s, p] = prob
            mixed = dot_nn(qkv_t[2 * hd + p * 2 * DH : 2 * hd + (p + 1) * 2 * DH, part], prob.astype(BF16))
            o_t[rows, part] = jnp.concatenate(
                [mixed[:DH, :length], mixed[DH:, length:]], axis=0
            ).astype(BF16)
        return carry

    lax.fori_loop(0, seqs, attend, 0)

    def feed(c, carry):
        part = pl.ds(pl.multiple_of(c * chunk, chunk), chunk)
        m = x_t[:, part].astype(F32) + dot_nn(wo_t[...], o_t[:, part])
        scale = lax.rsqrt(jnp.mean(m * m, axis=0, keepdims=True) + EPSILON)
        z = m * scale
        normed = (z * g2_col).astype(BF16)
        c_t[:, part] = normed
        dy = dy_t[:, part]
        u = dot_nn(win_t[...], normed)
        value, slope = gelu_parts(u)
        act = value.astype(BF16)
        act_t[:, part] = act
        du = (dot_nn(wout[...], dy) * slope).astype(BF16)
        du_t[:, part] = du
        y = m + dot_nn(wout_t[...], act)
        for k in range(chunk // length):
            y_out[c * (chunk // length) + k] = y[:, k * length : (k + 1) * length].T.astype(BF16)
        dc = dot_nn(win[...], du)
        gain = dc * z
        for k in range(chunk // length):
            g2_acc[...] += gain[:, k * length : (k + 1) * length]
        e = dc * g2_col
        dm = dy.astype(F32) + scale * (e - z * jnp.mean(e * z, axis=0, keepdims=True))
        dm_t[:, part] = dm
        low = dm.astype(BF16)
        dmb_t[:, part] = low
        do_t[:, part] = dot_nn(wo[...], low).astype(BF16)
        return carry

    lax.fori_loop(0, chunks, feed, 0)

    def attend_back(s, carry):
        part = pl.ds(pl.multiple_of(s * length, length), length)
        for p in range(pairs):
            rows = slice(p * 2 * DH, (p + 1) * 2 * DH)
            krows = slice(hd + p * 2 * DH, hd + (p + 1) * 2 * DH)
            vrows = slice(2 * hd + p * 2 * DH, 2 * hd + (p + 1) * 2 * DH)
            do2 = split_pair(do_t[rows, part])
            q2 = split_pair(qkv_t[rows, part])
            prob = p_s[s, p]
            dprob = dot_nn(kv[part, krows], do2)
            ds = prob * (dprob - jnp.sum(dprob * prob, axis=0, keepdims=True))
            dsum[p] += ds
            low = ds.astype(BF16)
            dqkv_t[vrows, part] = dot_nt(do2, prob.astype(BF16)).astype(BF16)
            dqkv_t[krows, part] = dot_nt(q2, low).astype(BF16)
            dq = dot_nn(qkv_t[krows, part], low) * (1.0 / math.sqrt(DH))
            dqkv_t[rows, part] = jnp.concatenate(
                [dq[:DH, :length], dq[DH:, length:]], axis=0
            ).astype(BF16)
        return carry

    lax.fori_loop(0, seqs, attend_back, 0)

    def inputs_back(c, carry):
        part = pl.ds(pl.multiple_of(c * chunk, chunk), chunk)
        xf, scale = norm_one(c)
        z = xf * scale
        da = dot_nn(wqkv[...], dqkv_t[:, part])
        gain = da * z
        for k in range(chunk // length):
            g1_acc[...] += gain[:, k * length : (k + 1) * length]
        e = da * g1_col
        ig = dm_t[:, part] + scale * (e - z * jnp.mean(e * z, axis=0, keepdims=True))
        igb_t[:, part] = ig.astype(BF16)
        for k in range(chunk // length):
            ig_out[c * (chunk // length) + k] = ig[:, k * length : (k + 1) * length].T
        return carry

    lax.fori_loop(0, chunks, inputs_back, 0)

    def to_slots(k, carry):
        first = pl.multiple_of(k * cap2, cap2)
        slots_out[pl.ds(first, cap2), :] = dot_nt(
            hot_slots(pos[...], first, cap2), igb_t[...]
        ).astype(BF16)
        return carry

    lax.fori_loop(0, slots_out.shape[0] // cap2, to_slots, 0)

    at = 0
    for k in range(3 * hd // width):
        block = slice(k * width, (k + 1) * width)
        w_out[at : at + width, :] = dot_nt(a_t[...], dqkv_t[block, :]).astype(BF16)
        at += width
    for k in range(ff // width):
        block = slice(k * width, (k + 1) * width)
        w_out[at : at + width, :] = dot_nt(c_t[...], du_t[block, :]).astype(BF16)
        at += width
    w_out[at : at + hd, :] = dot_nt(o_t[...], dmb_t[...]).astype(BF16)
    at += hd
    w_out[at : at + ff, :] = dot_nt(act_t[...], dy_t[...]).astype(BF16)
    at += ff
    if at < w_out.shape[0]:
        w_out[at:, :] = jnp.zeros((w_out.shape[0] - at, width), BF16)

    def bias_back(r, carry):
        part = pl.ds(pl.multiple_of(r * 8, 8), 8)
        bt = buck_t[part, :]
        grads = [dsum[h // 2, part, (h % 2) * length : (h % 2 + 1) * length] for h in range(heads)]
        for b in range(bucket_count):
            here = bt == float(b)
            for h in range(heads):
                b_acc[h, b] += jnp.where(here, grads[h], 0.0)
        return carry

    lax.fori_loop(0, length // 8, bias_back, 0)
    small_out[...] = jnp.zeros_like(small_out)
    small_out[0:1, :] = jnp.sum(g1_acc[...].T, axis=0, keepdims=True)
    small_out[1:2, :] = jnp.sum(g2_acc[...].T, axis=0, keepdims=True)
    for h in range(heads):
        by_bucket = jnp.sum(b_acc[h], axis=1)
        small_out[2 + h : 3 + h, 0:bucket_count] = jnp.sum(by_bucket.T, axis=0, keepdims=True)


def exchange_body(
    n, lo, cap, slots, w_in, small_in,
    inc, w_tot, small_tot,
    core_buf, half, lo_buf, quarter, hi_buf, small_a, small_b, small_c,
    row_send, row_recv, fwd_send, fwd_recv, core_sem, lo_send, lo_recv, hi_send, hi_recv,
    sa_sem, sb_send, sb_recv, sc_send, sc_recv, gh_send, gh_recv, gl_send, gl_recv, gc_send, gc_recv,
):
    me = lax.axis_index("emb")
    core = lax.axis_index("dp")
    hi = n // lo
    my_hi = me // lo
    my_lo = lax.rem(me, lo)
    half_rows, lo_rows, hi_rows = half.shape[0], quarter.shape[0], hi_buf.shape[1]

    barrier = pltpu.get_barrier_semaphore()

    def greet(k, carry):
        pl.semaphore_signal(
            barrier, inc=1, device_id={"emb": lax.rem(me + k, n)}, device_id_type=MESH
        )
        return carry

    lax.fori_loop(1, n, greet, 0)
    pl.semaphore_signal(barrier, inc=1, device_id={"dp": 1 - core}, device_id_type=MESH)
    pl.semaphore_wait(barrier, n)

    def block_at(j):
        return pl.ds(pl.multiple_of(j * cap, cap), cap)

    def remote(src, dst, send_sem, recv_sem, device):
        return pltpu.make_async_remote_copy(
            src_ref=src, dst_ref=dst, send_sem=send_sem, recv_sem=recv_sem,
            device_id=device, device_id_type=MESH,
        )

    def to_core(src, dst, send_sem, recv_sem):
        return remote(src, dst, send_sem, recv_sem, {"dp": 1 - core})

    theirs = pl.ds(pl.multiple_of((1 - core) * half_rows, half_rows), half_rows)
    mine = pl.ds(pl.multiple_of(core * half_rows, half_rows), half_rows)
    swap = to_core(w_in.at[theirs], core_buf, core_sem.at[0], core_sem.at[1])
    swap.start()
    small_a[core] = small_in[...]
    swap_small = to_core(small_a.at[core], small_a.at[core], sa_sem.at[0], sa_sem.at[1])
    swap_small.start()

    def row_copy(j):
        back = lax.rem(n - j, n)
        return remote(
            slots.at[block_at(j)], inc.at[core, block_at(back)],
            row_send.at[j], row_recv.at[back], {"emb": lax.rem(me + j, n)},
        )

    def row_arrival(j):
        return remote(
            slots.at[block_at(j)], inc.at[core, block_at(j)],
            row_send.at[j], row_recv.at[j], {"emb": lax.rem(me + j, n)},
        )

    def forward(j):
        return to_core(
            inc.at[core, block_at(j)], inc.at[core, block_at(j)], fwd_send.at[j], fwd_recv.at[j]
        )

    def forwarded(j):
        return to_core(
            inc.at[core, block_at(j)], inc.at[1 - core, block_at(j)], fwd_send.at[j], fwd_recv.at[j]
        )

    def row_start(j, carry):
        row_copy(j).start()
        return carry

    lax.fori_loop(1, n, row_start, 0)
    inc[core, 0:cap, :] = slots[0:cap, :]
    forward(0).start()

    swap.wait()
    swap_small.wait()

    def add_half(r, carry):
        at = pl.multiple_of(r * hi_rows, hi_rows)
        total = w_in[pl.ds(pl.multiple_of(core * half_rows + at, hi_rows), hi_rows), :].astype(F32)
        half[pl.ds(at, hi_rows), :] = (total + core_buf[pl.ds(at, hi_rows), :].astype(F32)).astype(
            BF16
        )
        return carry

    lax.fori_loop(0, half_rows // hi_rows, add_half, 0)
    small_b[my_lo] = small_a[0] + small_a[1]

    def lo_peer(k):
        return lax.rem(my_lo + k, lo)

    def lo_copy(k):
        peer = lo_peer(k)
        return remote(
            half.at[pl.ds(pl.multiple_of(peer * lo_rows, lo_rows), lo_rows)], lo_buf.at[lo - k],
            lo_send.at[k], lo_recv.at[lo - k], {"emb": my_hi * lo + peer},
        )

    def lo_arrival(k):
        return remote(
            quarter, lo_buf.at[k], lo_send.at[k], lo_recv.at[k], {"emb": my_hi * lo + lo_peer(k)}
        )

    def small_lo(k):
        return remote(
            small_b.at[my_lo], small_b.at[my_lo], sb_send.at[k], sb_recv.at[lo - k],
            {"emb": my_hi * lo + lo_peer(k)},
        )

    def small_lo_arrival(k):
        return remote(
            small_b.at[my_lo], small_b.at[lo_peer(k)], sb_send.at[k], sb_recv.at[k],
            {"emb": my_hi * lo + lo_peer(k)},
        )

    for k in range(1, lo):
        lo_copy(k).start()
        small_lo(k).start()
    for k in range(1, lo):
        lo_arrival(k).wait_recv()
        small_lo_arrival(k).wait_recv()

    def add_lo(r, carry):
        at = pl.multiple_of(r * hi_rows, hi_rows)
        total = half[pl.ds(pl.multiple_of(my_lo * lo_rows + at, hi_rows), hi_rows), :].astype(F32)
        for k in range(1, lo):
            total = total + lo_buf[k, pl.ds(at, hi_rows), :].astype(F32)
        quarter[pl.ds(at, hi_rows), :] = total.astype(BF16)
        return carry

    lax.fori_loop(0, lo_rows // hi_rows, add_lo, 0)
    total = small_b[0]
    for k in range(1, lo):
        total = total + small_b[k]
    small_c[my_hi] = total

    def hi_peer(k):
        return lax.rem(my_hi + k, hi)

    def hi_copy(k):
        peer = hi_peer(k)
        return remote(
            quarter.at[pl.ds(pl.multiple_of(peer * hi_rows, hi_rows), hi_rows)], hi_buf.at[hi - k],
            hi_send.at[k], hi_recv.at[hi - k], {"emb": peer * lo + my_lo},
        )

    def hi_arrival(k):
        return remote(
            hi_buf.at[k], hi_buf.at[k], hi_send.at[k], hi_recv.at[k], {"emb": hi_peer(k) * lo + my_lo}
        )

    def small_hi(k):
        return remote(
            small_c.at[my_hi], small_c.at[my_hi], sc_send.at[k], sc_recv.at[hi - k],
            {"emb": hi_peer(k) * lo + my_lo},
        )

    def small_hi_arrival(k):
        return remote(
            small_c.at[my_hi], small_c.at[hi_peer(k)], sc_send.at[k], sc_recv.at[k],
            {"emb": hi_peer(k) * lo + my_lo},
        )

    for k in range(1, hi):
        hi_copy(k).start()
        small_hi(k).start()
    for k in range(1, hi):
        hi_arrival(k).wait_recv()
        small_hi_arrival(k).wait_recv()
    total = quarter[pl.ds(pl.multiple_of(my_hi * hi_rows, hi_rows), hi_rows), :].astype(F32)
    for k in range(1, hi):
        total = total + hi_buf[k].astype(F32)
    base = core * half_rows + my_lo * lo_rows

    def piece(h):
        return pl.ds(pl.multiple_of(base + h * hi_rows, hi_rows), hi_rows)

    def quarter_at(l):
        return pl.ds(pl.multiple_of(core * half_rows + l * lo_rows, lo_rows), lo_rows)

    def other_quarter_at(l):
        return pl.ds(pl.multiple_of((1 - core) * half_rows + l * lo_rows, lo_rows), lo_rows)

    w_tot[piece(my_hi), :] = total.astype(BF16)
    total = small_c[0]
    for k in range(1, hi):
        total = total + small_c[k]
    small_tot[...] = total

    def gather_hi(k):
        return remote(
            w_tot.at[piece(my_hi)], w_tot.at[piece(my_hi)], gh_send.at[k], gh_recv.at[hi - k],
            {"emb": hi_peer(k) * lo + my_lo},
        )

    def gather_hi_arrival(k):
        return remote(
            w_tot.at[piece(my_hi)], w_tot.at[piece(hi_peer(k))], gh_send.at[k], gh_recv.at[k],
            {"emb": hi_peer(k) * lo + my_lo},
        )

    def gather_lo(k):
        return remote(
            w_tot.at[quarter_at(my_lo)], w_tot.at[quarter_at(my_lo)], gl_send.at[k],
            gl_recv.at[lo - k], {"emb": my_hi * lo + lo_peer(k)},
        )

    def gather_lo_arrival(k):
        return remote(
            w_tot.at[quarter_at(my_lo)], w_tot.at[quarter_at(lo_peer(k))], gl_send.at[k],
            gl_recv.at[k], {"emb": my_hi * lo + lo_peer(k)},
        )

    def gather_core(l):
        return to_core(
            w_tot.at[quarter_at(l)], w_tot.at[quarter_at(l)], gc_send.at[l], gc_recv.at[l]
        )

    def gather_core_arrival(l):
        return to_core(
            w_tot.at[quarter_at(l)], w_tot.at[other_quarter_at(l)], gc_send.at[l], gc_recv.at[l]
        )

    for k in range(1, hi):
        gather_hi(k).start()
    for k in range(1, hi):
        gather_hi_arrival(k).wait_recv()
    for k in range(1, lo):
        gather_lo(k).start()
    gather_core(my_lo).start()

    def pass_on(j, carry):
        row_arrival(j).wait_recv()
        forward(j).start()
        return carry

    lax.fori_loop(1, n, pass_on, 0)
    for k in range(1, lo):
        gather_lo_arrival(k).wait_recv()
        gather_core(lo_peer(k)).start()
    for l in range(lo):
        gather_core_arrival(l).wait_recv()

    def rows_in(j, carry):
        forwarded(j).wait_recv()
        forward(j).wait_send()
        return carry

    lax.fori_loop(0, n, rows_in, 0)

    def rows_out(j, carry):
        row_copy(j).wait_send()
        return carry

    lax.fori_loop(1, n, rows_out, 0)
    for k in range(1, lo):
        lo_copy(k).wait_send()
        small_lo(k).wait_send()
        gather_lo(k).wait_send()
    for k in range(1, hi):
        hi_copy(k).wait_send()
        small_hi(k).wait_send()
        gather_hi(k).wait_send()
    for l in range(lo):
        gather_core(l).wait_send()


def scatter_body(
    n, cap, asked, inc, w_tot, small,
    grad, g1, wq, wk, wv, wo, bias, g2, win, wout,
    acc, wide, zero, out_sem,
):
    used = acc.shape[0]
    rows_dev = grad.shape[0]
    zero_rows = zero.shape[0]
    zero[...] = jnp.zeros_like(zero)

    def clear_copy(k):
        return pltpu.make_async_copy(
            zero, grad.at[pl.ds(used + k * zero_rows, zero_rows)], out_sem.at[3 + k]
        )

    spare = (rows_dev - used) // zero_rows
    for k in range(spare):
        clear_copy(k).start()

    def clear(r, carry):
        acc[pl.ds(pl.multiple_of(r * 256, 256), 256), :] = jnp.zeros((256, acc.shape[1]), F32)
        return carry

    lax.fori_loop(0, used // 256, clear, 0)

    for c in range(2):
        def source(j, carry):
            part = pl.ds(pl.multiple_of(j * cap, cap), cap)
            wide[part, :] = inc[c, part, :].astype(F32)

            def eight(k, inner):
                for r in range(8):
                    at = asked[c, j, 0, k * 8 + r] & (LIVE - 1)
                    acc[pl.ds(at, 1), :] += wide[pl.ds(j * cap + k * 8 + r, 1), :]
                return inner

            lax.fori_loop(0, (asked[c, j, 1, 0] + 7) // 8, eight, 0)
            return carry

        lax.fori_loop(0, n, source, 0)

    third = used // 3

    def out_copy(k):
        part = pl.ds(k * third, third)
        return pltpu.make_async_copy(acc.at[part], grad.at[part], out_sem.at[k])

    for k in range(3):
        out_copy(k).start()

    width = wq.shape[0]
    hd = wq.shape[1]
    ff = win.shape[1]
    at = 0
    for ref in (wq, wk, wv, win):
        for k in range(ref.shape[1] // width):
            ref[:, k * width : (k + 1) * width] = w_tot[at : at + width, :].astype(F32)
            at += width
    wo[...] = w_tot[at : at + hd, :].astype(F32)
    at += hd
    wout[...] = w_tot[at : at + ff, :].astype(F32)
    g1[...] = small[0:1, :]
    g2[...] = small[1:2, :]
    heads, buckets = bias.shape
    bias[...] = small[2 : 2 + heads, 0:buckets]
    for k in range(3):
        out_copy(k).wait()
    for k in range(spare):
        clear_copy(k).wait()


def on_device(
    hashed_ids, owners, domain_tags, user_counts, lengths, buckets, table, gain_one,
    query_weight_matrix, key_weight_matrix, value_weight_matrix, attention_output_weight,
    bias_table, gain_two, feedforward_input_weight, feedforward_output_weight, cotangent,
):
    n = lax.axis_size("emb")
    seqs, length = hashed_ids.shape
    tokens = seqs * length
    rows_dev, width = table.shape
    used = 3 * (rows_dev // 4)
    cap = max(2, 2 * tokens // n)
    hd = query_weight_matrix.shape[1]
    ff = feedforward_input_weight.shape[1]
    heads = hd // DH
    pairs = heads // 2
    bucket_count = bias_table.shape[0]
    slots = n * cap
    lo = 2 ** ((n.bit_length()) // 2)
    hi = n // lo
    unit = 2 * n * 16
    w_rows = 4 * hd + 2 * ff
    w_rows = -(-w_rows // unit) * unit
    vmem = pl.BlockSpec(memory_space=pltpu.VMEM)
    smem = pl.BlockSpec(memory_space=pltpu.SMEM)
    anywhere = pl.BlockSpec(memory_space=pl.ANY)
    dma = pltpu.SemaphoreType.DMA
    shape = jax.ShapeDtypeStruct

    x_t, pos, asked = pl.pallas_call(
        functools.partial(lookup_body, n, cap, used),
        out_shape=(
            shape((width, tokens), BF16),
            shape((seqs, length), jnp.int32),
            shape((2, n, 2, LANES), jnp.int32),
        ),
        in_specs=[vmem, vmem, smem, smem, smem, anywhere],
        out_specs=(vmem, vmem, vmem),
        scratch_shapes=[
            pltpu.VMEM((n, 1, LANES), jnp.int32),
            pltpu.VMEM((n, 1, LANES), jnp.int32),
            pltpu.SMEM((n, 1, LANES), jnp.int32),
            pltpu.VMEM((used, width), BF16),
            pltpu.VMEM((used, width), F32),
            pltpu.VMEM((cap, width), F32),
            pltpu.VMEM((slots, width), BF16),
            pltpu.VMEM((slots, width), BF16),
            pltpu.VMEM((width, tokens), F32),
            dma((n,)), dma((n,)), dma((n,)), dma((n,)), dma, dma, dma((6,)), dma,
        ],
        compiler_params=pltpu.CompilerParams(
            collective_id=0, has_side_effects=True, vmem_limit_bytes=VMEM_LIMIT
        ),
        name="lookup",
    )(hashed_ids, owners.reshape(seqs, length), domain_tags, user_counts, lengths, table)

    output, input_grad, slot_grads, w_part, small_part = pl.pallas_call(
        functools.partial(block_body, 256),
        out_shape=(
            shape((seqs, length, width), BF16),
            shape((seqs, length, width), F32),
            shape((slots, width), BF16),
            shape((w_rows, width), BF16),
            shape((8, LANES), F32),
        ),
        in_specs=[smem, smem] + [vmem] * 12,
        out_specs=(vmem,) * 5,
        scratch_shapes=[
            pltpu.VMEM((3 * hd, width), BF16),
            pltpu.VMEM((width, 3 * hd), BF16),
            pltpu.VMEM((width, hd), BF16),
            pltpu.VMEM((ff, width), BF16),
            pltpu.VMEM((width, ff), BF16),
            pltpu.VMEM((length, length), F32),
            pltpu.VMEM((pairs, length, 2 * length), F32),
            pltpu.VMEM((width, tokens), BF16),
            pltpu.VMEM((3 * hd, tokens), BF16),
            pltpu.VMEM((tokens, 2 * hd), BF16),
            pltpu.VMEM((seqs, pairs, length, 2 * length), F32),
            pltpu.VMEM((hd, tokens), BF16),
            pltpu.VMEM((width, tokens), BF16),
            pltpu.VMEM((ff, tokens), BF16),
            pltpu.VMEM((ff, tokens), BF16),
            pltpu.VMEM((width, tokens), BF16),
            pltpu.VMEM((width, tokens), F32),
            pltpu.VMEM((width, tokens), BF16),
            pltpu.VMEM((hd, tokens), BF16),
            pltpu.VMEM((3 * hd, tokens), BF16),
            pltpu.VMEM((pairs, length, 2 * length), F32),
            pltpu.VMEM((width, tokens), BF16),
            pltpu.VMEM((width, length), F32),
            pltpu.VMEM((width, length), F32),
            pltpu.VMEM((heads, bucket_count, 8, length), F32),
        ],
        compiler_params=pltpu.CompilerParams(vmem_limit_bytes=VMEM_LIMIT),
        name="block",
    )(
        lengths, bias_table.T, buckets, x_t, cotangent, gain_one.reshape(1, width),
        query_weight_matrix, key_weight_matrix, value_weight_matrix, attention_output_weight,
        gain_two.reshape(1, width), feedforward_input_weight, feedforward_output_weight, pos,
    )

    incoming, w_total, small_total = pl.pallas_call(
        functools.partial(exchange_body, n, lo, cap),
        out_shape=(
            shape((2, slots, width), BF16),
            shape((w_rows, width), BF16),
            shape((8, LANES), F32),
        ),
        in_specs=[vmem] * 3,
        out_specs=(vmem,) * 3,
        scratch_shapes=[
            pltpu.VMEM((w_rows // 2, width), BF16),
            pltpu.VMEM((w_rows // 2, width), BF16),
            pltpu.VMEM((lo, w_rows // 2 // lo, width), BF16),
            pltpu.VMEM((w_rows // 2 // lo, width), BF16),
            pltpu.VMEM((hi, w_rows // 2 // n, width), BF16),
            pltpu.VMEM((2, 8, LANES), F32),
            pltpu.VMEM((lo, 8, LANES), F32),
            pltpu.VMEM((hi, 8, LANES), F32),
            dma((n,)), dma((n,)), dma((n,)), dma((n,)), dma((2,)),
            dma((lo,)), dma((lo,)), dma((hi,)), dma((hi,)), dma((2,)),
            dma((lo,)), dma((lo,)), dma((hi,)), dma((hi,)),
            dma((hi,)), dma((hi,)), dma((lo,)), dma((lo,)), dma((lo,)), dma((lo,)),
        ],
        compiler_params=pltpu.CompilerParams(
            collective_id=1, has_side_effects=True, vmem_limit_bytes=VMEM_LIMIT
        ),
        name="exchange",
    )(slot_grads, w_part, small_part)

    zero_rows = min(1024, rows_dev - used)
    table_grad, g1, gq, gk, gv, go, gb, g2, gin, gout = pl.pallas_call(
        functools.partial(scatter_body, n, cap),
        out_shape=(
            shape((rows_dev, width), F32),
            shape((1, width), F32),
            shape((width, hd), F32),
            shape((width, hd), F32),
            shape((width, hd), F32),
            shape((hd, width), F32),
            shape((heads, bucket_count), F32),
            shape((1, width), F32),
            shape((width, ff), F32),
            shape((ff, width), F32),
        ),
        in_specs=[smem, vmem, vmem, vmem],
        out_specs=(anywhere,) + (vmem,) * 9,
        scratch_shapes=[
            pltpu.VMEM((used, width), F32),
            pltpu.VMEM((slots, width), F32),
            pltpu.VMEM((zero_rows, width), F32),
            dma((3 + (rows_dev - used) // zero_rows,)),
        ],
        compiler_params=pltpu.CompilerParams(vmem_limit_bytes=VMEM_LIMIT),
        name="scatter",
    )(asked, incoming, w_total, small_total)
    return (
        output, input_grad, table_grad, g1.reshape(width), gq, gk, gv, go, gb.T, g2.reshape(width),
        gin, gout,
    )


def solution(mesh):
    split = ("emb", "dp")
    return jax.shard_map(
        on_device,
        mesh=mesh,
        in_specs=(
            P(split, None), P(split, None, None), P(split), P(), P(split, None), P(),
            P("emb", None), P(), P(), P(), P(), P(), P(), P(), P(), P(), P(split, None, None),
        ),
        out_specs=(
            P(split, None, None), P(split, None, None), P("emb", None), P(), P(), P(), P(), P(),
            P(), P(), P(), P(),
        ),
        check_vma=False,
    )
```

time: 348 us -> 115 us (0.33)
  the two profiles are of different devices: /device:TPU:27 before, /device:TPU:19 now
where the time goes in v1:
time: 115 us; the launch traced here: 114 us
  Pallas kernels  113 us (98%)
    pallas_call x1, Pallas kernels, on_device(): pl.pallas_call(functools.partial(exchange_body, n, lo, cap), out_shape=(s...  39.3 us
    pallas_call x1, Pallas kernels, on_device(): pl.pallas_call(functools.partial(block_body, 256), out_shape=(shape((seqs...  29.8 us
    pallas_call x1, Pallas kernels, on_device(): pl.pallas_call(functools.partial(lookup_body, n, cap, used), out_shape=(s...  23.7 us
    pallas_call x1, Pallas kernels, on_device(): pl.pallas_call(functools.partial(scatter_body, n, cap), out_shape=(shape(...  20.4 us

profile of v1, /device:TPU:19, one launch (start us, length us, event | category | flops | bytes accessed | tf_op | source)
XLA Modules:
  0.0 114.0 jit_solution(16476294634418707586)
XLA Ops:
  0.6 23.7 %lookup.1 = (bf16[128,1024]{1,0:T(8,128)(2,1)}, s32[8,128]{1,0:T(8,128)}, s32[2,16,2,128]{3,2,1,0:T(2,128)}) custom-call(s32[8,128]{1,0:T(8,128)} %ids.1, s32[8,128]{1,0:T(8,128)} %bitcast.7, s32[8]{0:T(128)} %tags.1, s32[3]{0:T(128)} %counts.1, s32[1,8]{1,0:T(1,128)} %lens.3, bf16[32768,128]{1,0:T(8,128)(2,1)} %table.1), custom_call_target="tpu_custom_call" | custom-call | tf_op jit(solution)/shard_map/lookup/pallas_call | solution.py:850
  24.4 29.8 %block.1 = (bf16[8,128,128]{2,1,0:T(8,128)(2,1)}, f32[8,128,128]{2,1,0:T(8,128)}, bf16[2048,128]{1,0:T(8,128)(2,1)}, bf16[3584,128]{1,0:T(8,128)(2,1)}, f32[8,128]{1,0:T(8,128)}) custom-call(s32[1,8]{1,0:T(1,128)} %lens.3, f32[6,32]{1,0:T(8,128)} %bitcast.8, s32[128,128]{1,0:T(8,128)} %buckets.1, bf16[128,1024]{1,0:T(8,128)(2,1)} %get-tuple-element.33.x_t, ...), custom_call_target="tpu_custom_call" | custom-call | tf_op jit(solution)/shard_map/block/pallas_call | solution.py:877
  54.2 39.3 %exchange.1 = (bf16[2,2048,128]{2,1,0:T(8,128)(2,1)}, bf16[3584,128]{1,0:T(8,128)(2,1)}, f32[8,128]{1,0:T(8,128)}) custom-call(bf16[2048,128]{1,0:T(8,128)(2,1)} %get-tuple-element.38.slots, bf16[3584,128]{1,0:T(8,128)(2,1)} %get-tuple-element.39.w_in, f32[8,128]{1,0:T(8,128)} %get-tuple-element.40.small_in), custom_call_target="tpu_custom_call" | custom-call | tf_op jit(solution)/shard_map/exchange/pallas_call | solution.py:923
  93.5 20.4 %scatter.1 = (f32[32768,128]{1,0:T(8,128)}, f32[1,128]{1,0:T(1,128)}, f32[128,384]{1,0:T(8,128)}, f32[128,384]{1,0:T(8,128)}, f32[128,384]{1,0:T(8,128)}, /*inde...) custom-call(s32[2,16,2,128]{3,2,1,0:T(2,128)} %get-tuple-element.37.asked, ...), custom_call_target="tpu_custom_call" | custom-call | tf_op jit(solution)/shard_map/scatter/pallas_call | solution.py:953
